TPU v7x, 32 devices: a whole 2x2x4 slice. The times are simulated.
32 devices in a mesh: bead: 8 (over z, y), space: 4 (over x, core).
Axes of the slice: x: 2, y: 2, z: 4, core: 2. Of those that a mesh axis runs over, the one named last changes fastest.
Arguments:
- positions: float32 [8, 3, 65536], P('bead', None, 'space'), may hold values from -5.5 to 5.5
- charges: float32 [65536], P('space'), may hold values from -1 to 1
- polarizability: float32 [65536], P('space'), may hold values from 0.03 to 0.12
- masses: float32 [65536], P('space'), may hold values from 1 to 16
- neighbors: int32 [512, 8], P('space'), may hold values from 0 to 135, as said below
Outputs:
- forces: float32 [8, 3, 65536], P('bead', None, 'space')
- dipoles: float32 [3, 65536], P(None, ('space', 'bead'))
Inputs may be any that keep to these rules, and one draw needn't show every extreme that they name: `neighbors`: row t lists 8 different tiles by their index in its domain's extended numbering: the last 4 tiles of the previous domain, the domain's own 128 tiles, the first 4 tiles of the next domain (domains form a cycle). Every listed tile lies within 4 tiles of tile t, and the two tiles at distance exactly 4 on either side are always listed.
All inputs are finite; a program needn't handle non-finite values.
Results may differ from a plain program's by a relative error of at most 0.0001.
Values sent between devices are 32-bit elements; how exact they have to be, the bound alone decides.
A program may use at most 64 MiB of HBM per device.

v0:
```python
import math

import jax
import jax.numpy as jnp
from jax import lax
from jax.sharding import PartitionSpec as P

TILE = 128
HALO_T = 4
ITERS = 3


REPULSION = 0.2
SPRING = 0.1


def shifted(block, axis, distance):
    devices = range(lax.axis_size(axis))
    route = [((i - distance) % len(devices), i) for i in devices]
    return lax.ppermute(block, axis, route)


def extended_2(value, sides, width):
    for axis, dim in sides:
        size, length = (lax.axis_size(axis), value.shape[dim])
        up = [(i, (i + 1) % size) for i in range(size)]
        down = [(j, i) for i, j in up]
        last = lax.slice_in_dim(value, length - width, length, axis=dim)
        first = lax.slice_in_dim(value, 0, width, axis=dim)
        before = lax.ppermute(last, axis, up)
        after = lax.ppermute(first, axis, down)
        value = jnp.concatenate([before, value, after], axis=dim)
    return value


def repulsion_kernel(targets, sources):
    displace = targets[:, :, :, None] - sources[:, :, None, :]
    weight = jnp.exp(-0.5 * jnp.sum(displace * displace, axis=0))
    return REPULSION * jnp.sum(weight[None] * displace, axis=3)


def charge_kernel(targets, sources, charge):
    displace = targets[:, :, :, None] - sources[:, :, None, :]
    weight = jnp.exp(-0.25 * jnp.sum(displace * displace, axis=0)) * charge[0][:, None, :]
    return jnp.sum(weight[None] * displace, axis=3)


def dipole_kernel(targets, sources, dipole):
    displace = targets[:, :, :, None] - sources[:, :, None, :]
    weight = jnp.exp(-0.25 * jnp.sum(displace * displace, axis=0))
    spread_dip = dipole[:, :, None, :]
    projected = jnp.sum(displace * spread_dip, axis=0)
    return jnp.sum(weight[None] * (0.25 * displace * projected[None] - 0.5 * spread_dip), axis=3)


def grouped(kernel, targets, sources):
    tile_count = targets.shape[1]
    group_size = math.gcd(tile_count, 4)

    def split_tiles(tensor):
        return jnp.moveaxis(
            tensor.reshape(tensor.shape[0], tile_count // group_size, group_size, tensor.shape[2]),
            1,
            0,
        )

    pieces = tuple((split_tiles(tensor) for tensor in (targets,) + tuple(sources)))
    result = lax.map(lambda member: kernel(*member), pieces)
    return jnp.moveaxis(result, 0, 1).reshape(3, tile_count, targets.shape[2])


def gather_local(extended, tile_rows):
    channels = extended.shape[0]
    tiles = extended.reshape(channels, extended.shape[1] // TILE, TILE)
    picked = jnp.take(tiles, tile_rows, axis=1)
    return picked.reshape(channels, tile_rows.shape[0], tile_rows.shape[1] * TILE)


def cycle_extend(field, rim_width):
    bead_index = lax.axis_index("bead")
    beads = lax.axis_size("bead")
    tail_part = field[:, field.shape[1] - rim_width :]
    head_part = field[:, :rim_width]
    from_lower = shifted(tail_part, "bead", 1)
    lower_far = shifted(from_lower, "space", 1)
    from_upper = shifted(head_part, "bead", -1)
    upper_far = shifted(from_upper, "space", -1)
    lower_rim = jnp.where(bead_index == 0, lower_far, from_lower)
    upper_rim = jnp.where(bead_index == beads - 1, upper_far, from_upper)
    return jnp.concatenate([lower_rim, field, upper_rim], axis=1)


def per_device(positions, charges, polarizability, masses, neighbors):
    coords = positions[0]
    atom_dev = coords.shape[1]
    rim_width = HALO_T * TILE
    tiles_domain = atom_dev // TILE
    beads = lax.axis_size("bead")
    bead_index = lax.axis_index("bead")
    own_tiles = tiles_domain // beads
    own_start = bead_index * own_tiles
    cycle_rows = extended_2(positions, (("bead", 0),), 1)
    spring = SPRING * masses[None, :] * (cycle_rows[0] + cycle_rows[2] - 2.0 * coords)
    extended = extended_2(coords, (("space", 1),), rim_width)
    targets = coords.reshape(3, tiles_domain, TILE)
    short_range = grouped(repulsion_kernel, targets, (gather_local(extended, neighbors),)).reshape(
        3, atom_dev
    )
    own_share = lax.psum_scatter(coords, "bead", scatter_dimension=1, tiled=True) / beads
    own_alpha = lax.dynamic_slice_in_dim(polarizability, own_start * TILE, own_tiles * TILE, 0)
    own_charge = lax.dynamic_slice_in_dim(charges, own_start * TILE, own_tiles * TILE, 0)
    with_charge = jnp.concatenate([own_share, own_charge[None]], axis=0)
    cent_ext = cycle_extend(with_charge, rim_width)
    own_rows = lax.dynamic_slice_in_dim(neighbors, own_start, own_tiles, 0) - own_start
    cent_sources = gather_local(cent_ext[:3], own_rows)
    charge_sources = gather_local(cent_ext[3:], own_rows)
    own_targets = own_share.reshape(3, own_tiles, TILE)
    permanent = grouped(charge_kernel, own_targets, (cent_sources, charge_sources)).reshape(
        3, own_tiles * TILE
    )

    def induced(dipole_own):
        wide_dip = cycle_extend(dipole_own, rim_width)
        field = grouped(
            dipole_kernel, own_targets, (cent_sources, gather_local(wide_dip, own_rows))
        )
        return field.reshape(3, own_tiles * TILE)

    dipoles = own_alpha[None] * permanent
    for sweep_index in range(ITERS):
        dipoles = own_alpha[None] * (permanent + induced(dipoles))
    pulled_own = own_charge[None] * induced(dipoles)
    pulled = lax.all_gather(pulled_own, "bead", axis=1, tiled=True)
    forces = (short_range + spring + pulled)[None]
    return (forces, dipoles)


def solution(mesh):
    in_specs = (P("bead", None, "space"), P("space"), P("space"), P("space"), P("space", None))
    out_specs = (P("bead", None, "space"), P(None, ("space", "bead")))
    return jax.shard_map(
        per_device, mesh=mesh, in_specs=in_specs, out_specs=out_specs, check_vma=False
    )
```

profile of v0, /device:TPU:0, one launch (start us, length us, event | category | flops | bytes accessed | tf_op | source)
XLA Modules:
  0.0 421.9 jit_solution(12408635066285397937)
XLA Ops:
  8.3 5.1 %copy.155 = f32[3,16384]{0,1:T(8,128)} copy(f32[3,16384]{1,0:T(4,128)S(1)} %bitcast.188) | data formatting | bytes 393216
  13.4 3.0 collective-permute-start.2
  16.4 3.1 collective-permute-start.3
  20.2 145.0 %reduce-scatter.4.cloned.1.call-done = f32[2048,3]{1,0:T(8,128)} async-done(((f32[16384,3]{1,0:T(8,128)}), f32[2048,3]{1,0:T(8,128)}) %reduce-scatter.4.cloned.1.call-update) | async-done | bytes 24592
  168.6 3.3 collective-permute-start.6
  174.2 1.8 collective-permute-start.7
  179.1 7.7 %while.61 = (s32[]{:T(128)}, f32[4,3,4,128]{3,2,1,0:T(4,128)S(1)}, f32[4,3,4,128]{3,2,1,0:T(4,128)S(1)}, f32[4,3,4,1024]{3,2,1,0:T(4,128)S(1)}, f32[4,1,4,1024]{3,2,1,0:T(4,128)S(1)}, /*index=5*/s32[]{:T(128)}) while((s32[]{:T(128)}, f32[4,3,4,128]{3,2,1,0:T(4,128)S(1)}, f32[4,3,4,128]{3,2,1,0:T(4,128)S(1)}, f32[4,3,4,1024]{3,2,1,0:T(4,128)S(1)}, ...), condition=%wide.region_8.10_spmd, body=%wide.region_5.9_spmd.sunk | while | flops 9959938 | bytes 8677461 | solution.py:68
  187.0 1.6 collective-permute-start
  188.6 4.4 %collective-permute-start.10 = (f32[3,512]{1,0:T(4,128)S(1)}, f32[3,512]{1,0:T(4,128)S(1)}, u32[]{:S(2)}, u32[]{:S(2)}) collective-permute-start(f32[3,512]{1,0:T(4,128)S(1)} %get-tuple-element.354), channel_id=1, source_target_pairs={{4,0},{8,4},{12,8},{16,12},{20,16},{24,20},{28,24},{0,28},{5,1},{9... | collective-permute-start | bytes 18440 | tf_op jit(solution)/shard_map/ppermute | solution.py:20
  197.5 14.6 %while.62 = (s32[]{:T(128)}, f32[4,3,4,128]{3,2,1,0:T(4,128)S(1)}, f32[4,3,4,128]{3,2,1,0:T(4,128)S(1)}, f32[4,3,4,1024]{3,2,1,0:T(4,128)S(1)}, f32[4,3,4,1024]{3,2,0,1:T(4,128)S(1)}, /*index=5*/s32[]{:T(128)}) while((s32[]{:T(128)}, f32[4,3,4,128]{3,2,1,0:T(4,128)S(1)}, f32[4,3,4,128]{3,2,1,0:T(4,128)S(1)}, ...), condition=%wide.region_13.15_spmd, body=%wide.region_9.14_spmd.sunk | while | flops 15739394 | bytes 17262676 | solution.py:68
  199.5 1.6 fusion.56
  203.2 1.6 fusion.56
  212.5 4.8 %collective-permute-start.14 = (f32[3,512]{1,0:T(4,128)S(1)}, f32[3,512]{1,0:T(4,128)S(1)}, u32[]{:S(2)}, u32[]{:S(2)}) collective-permute-start(f32[3,512]{1,0:T(4,128)S(1)} %get-tuple-element.352), channel_id=1, source_target_pairs={{4,0},{8,4},{12,8},{16,12},{20,16},{24,20},{28,24},{0,28},{5,1},{9... | collective-permute-start | bytes 18440 | tf_op jit(solution)/shard_map/ppermute | solution.py:20
  224.0 14.6 %while.63 = (s32[]{:T(128)}, f32[4,3,4,128]{3,2,1,0:T(4,128)S(1)}, f32[4,3,4,128]{3,2,1,0:T(4,128)S(1)}, f32[4,3,4,1024]{3,2,1,0:T(4,128)S(1)}, f32[4,3,4,1024]{3,2,0,1:T(4,128)S(1)}, /*index=5*/s32[]{:T(128)}) while((s32[]{:T(128)}, f32[4,3,4,128]{3,2,1,0:T(4,128)S(1)}, f32[4,3,4,128]{3,2,1,0:T(4,128)S(1)}, ...), condition=%wide.region_18.20_spmd, body=%wide.region_14.19_spmd.sunk | while | flops 15739394 | bytes 17262676 | solution.py:68
  226.1 1.6 fusion.58
  239.2 4.7 %collective-permute-start.18 = (f32[3,512]{1,0:T(4,128)S(1)}, f32[3,512]{1,0:T(4,128)S(1)}, u32[]{:S(2)}, u32[]{:S(2)}) collective-permute-start(f32[3,512]{1,0:T(4,128)S(1)} %get-tuple-element.350), channel_id=1, source_target_pairs={{4,0},{8,4},{12,8},{16,12},{20,16},{24,20},{28,24},{0,28},{5,1},{9... | collective-permute-start | bytes 18440 | tf_op jit(solution)/shard_map/ppermute | solution.py:20
  245.6 3.6 gather_fusion
  250.4 1.8 gather.16
  255.9 14.6 %while.64 = (s32[]{:T(128)}, f32[4,3,4,128]{3,2,1,0:T(4,128)S(1)}, f32[4,3,4,128]{3,2,1,0:T(4,128)S(1)}, f32[4,3,4,1024]{3,2,1,0:T(4,128)S(1)}, f32[4,3,4,1024]{3,2,0,1:T(4,128)S(1)}, /*index=5*/s32[]{:T(128)}) while((s32[]{:T(128)}, f32[4,3,4,128]{3,2,1,0:T(4,128)S(1)}, f32[4,3,4,128]{3,2,1,0:T(4,128)S(1)}, ...), condition=%wide.region_23.25_spmd, body=%wide.region_19.24_spmd.sunk | while | flops 15739394 | bytes 17262676 | solution.py:68
  270.8 1.7 select_bitcast_fusion
  272.5 4.7 %collective-permute-start.22 = (f32[3,512]{1,0:T(4,128)S(1)}, f32[3,512]{1,0:T(4,128)S(1)}, u32[]{:S(2)}, u32[]{:S(2)}) collective-permute-start(f32[3,512]{1,0:T(4,128)S(1)} %get-tuple-element.348), channel_id=1, source_target_pairs={{4,0},{8,4},{12,8},{16,12},{20,16},{24,20},{28,24},{0,28},{5,1},{9... | collective-permute-start | bytes 18440 | tf_op jit(solution)/shard_map/ppermute | solution.py:20
  278.2 86.0 %while.60 = (s32[]{:T(128)}, f32[32,3,4,128]{3,2,1,0:T(4,128)S(1)}, f32[32,3,4,128]{3,2,0,1:T(4,128)S(1)}, f32[32,3,4,1024]{3,2,0,1:T(4,128)}, s32[]{:T(128)}) while((s32[]{:T(128)}, f32[32,3,4,128]{3,2,1,0:T(4,128)S(1)}, f32[32,3,4,128]{3,2,0,1:T(4,128)S(1)}, f32[32,3,4,1024]{3,2,0,1:T(4,128)}, s32[]{:T(128)}) %tuple.187), condition=%wide.region_3.4_spmd, body=%wide.region_0.3_spmd.sunk | while | flops 9437186 | bytes 8628297 | solution.py:68
  367.5 14.6 %while.65 = (s32[]{:T(128)}, f32[4,3,4,128]{3,2,1,0:T(4,128)S(1)}, f32[4,3,4,128]{3,2,1,0:T(4,128)S(1)}, f32[4,3,4,1024]{3,2,1,0:T(4,128)S(1)}, f32[4,3,4,1024]{3,2,0,1:T(4,128)S(1)}, /*index=5*/s32[]{:T(128)}) while((s32[]{:T(128)}, f32[4,3,4,128]{3,2,1,0:T(4,128)S(1)}, f32[4,3,4,128]{3,2,1,0:T(4,128)S(1)}, ...), condition=%wide.region_28.30_spmd, body=%wide.region_24.29_spmd.sunk | while | flops 15739394 | bytes 17262676 | solution.py:68
  382.2 30.7 %all_gather.3 = f32[3,16384]{1,0:T(4,128)S(1)} all-gather(f32[3,2048]{1,0:T(4,128)S(1)} %broadcast_multiply_fusion.11), channel_id=1, replica_groups=mesh['bead'=8,'space'=4] {'bead'}, dimensions={1}, use_global_device_ids=true | all-gather | bytes 221184 | tf_op jit(solution)/shard_map/all_gather | solution.py:133
  (472 shorter events, 181.0 us)
Async XLA Ops:
  7.2 158.1 %reduce-scatter.4.cloned.1.call-start = ((), (), s32[]{:S(2)}) async-start(), calls=%async_computation.1 | async-start | bytes 9437184
  13.4 399.6 %collective-permute-start.2 = (f32[1,3,16384]{2,1,0:T(4,128)S(1)}, f32[1,3,16384]{2,1,0:T(4,128)S(1)}, u32[]{:S(2)}, u32[]{:S(2)}) collective-permute-start(f32[1,3,16384]{2,1,0:T(4,128)S(1)} %copy.187), channel_id=1, source_target_pairs={{0,4},{4,8},{8,12},{12,16},{16,20},{20,24},{24,28},{28,0},{1,5},{5... | collective-permute-start | bytes 589832 | tf_op jit(solution)/shard_map/ppermute | solution.py:30
  16.4 396.6 %collective-permute-start.3 = (f32[1,3,16384]{2,1,0:T(4,128)S(1)}, f32[1,3,16384]{2,1,0:T(4,128)}, u32[]{:S(2)}, u32[]{:S(2)}) collective-permute-start(f32[1,3,16384]{2,1,0:T(4,128)S(1)} %copy.187), channel_id=1, source_target_pairs={{4,0},{8,4},{12,8},{16,12},{20,16},{24,20},{28,24},{0,28},{5,1},{9... | collective-permute-start | bytes 589832 | tf_op jit(solution)/shard_map/ppermute | solution.py:31
  166.8 6.4 %collective-permute-start.4 = (f32[4,512]{1,0:T(4,128)S(1)}, f32[4,512]{1,0:T(4,128)S(1)}, u32[]{:S(2)}, u32[]{:S(2)}) collective-permute-start(f32[4,512]{1,0:T(4,128)S(1)} %get-tuple-element.345), channel_id=1, source_target_pairs={{28,0},{0,4},{4,8},{8,12},{12,16},{16,20},{20,24},{24,28},{29,1},{... | collective-permute-start | bytes 24584 | tf_op jit(solution)/shard_map/ppermute | solution.py:20
  168.6 5.6 %collective-permute-start.6 = (f32[4,512]{1,0:T(4,128)S(1)}, f32[4,512]{1,0:T(4,128)S(1)}, u32[]{:S(2)}, u32[]{:S(2)}) collective-permute-start(f32[4,512]{1,0:T(4,128)S(1)} %get-tuple-element.346), channel_id=1, source_target_pairs={{4,0},{8,4},{12,8},{16,12},{20,16},{24,20},{28,24},{0,28},{5,1},{9... | collective-permute-start | bytes 24584 | tf_op jit(solution)/shard_map/ppermute | solution.py:20
  173.2 3.1 collective-permute-start.5
  174.2 3.1 collective-permute-start.7
  186.9 6.4 %collective-permute-start.8 = (f32[3,512]{1,0:T(4,128)S(1)}, f32[3,512]{1,0:T(4,128)S(1)}, u32[]{:S(2)}, u32[]{:S(2)}) collective-permute-start(f32[3,512]{1,0:T(4,128)S(1)} %get-tuple-element.353), channel_id=1, source_target_pairs={{28,0},{0,4},{4,8},{8,12},{12,16},{16,20},{20,24},{24,28},{29,1},{... | collective-permute-start | bytes 18440 | tf_op jit(solution)/shard_map/ppermute | solution.py:20
  187.0 52.2 %collective-permute-start = (f32[3,512]{1,0:T(4,128)S(1)}, f32[3,512]{1,0:T(4,128)S(1)}, u32[]{:S(2)}, u32[]{:S(2)}) collective-permute-start(f32[3,512]{1,0:T(4,128)S(1)} %get-tuple-element.341), channel_id=1, source_target_pairs={{0,1},{1,2},{2,3},{3,0},{4,5},{5,6},{6,7},{7,4},{8,9},{9,10},{10,1... | collective-permute-start | bytes 18440 | tf_op jit(solution)/shard_map/ppermute | solution.py:30
  188.6 5.7 %collective-permute-start.10 = (f32[3,512]{1,0:T(4,128)S(1)}, f32[3,512]{1,0:T(4,128)S(1)}, u32[]{:S(2)}, u32[]{:S(2)}) collective-permute-start(f32[3,512]{1,0:T(4,128)S(1)} %get-tuple-element.354), channel_id=1, source_target_pairs={{4,0},{8,4},{12,8},{16,12},{20,16},{24,20},{28,24},{0,28},{5,1},{9... | collective-permute-start | bytes 18440 | tf_op jit(solution)/shard_map/ppermute | solution.py:20
  193.3 3.1 collective-permute-start.9
  194.3 2.2 collective-permute-start.11
  212.2 6.4 %collective-permute-start.12 = (f32[3,512]{1,0:T(4,128)S(1)}, f32[3,512]{1,0:T(4,128)S(1)}, u32[]{:S(2)}, u32[]{:S(2)}) collective-permute-start(f32[3,512]{1,0:T(4,128)S(1)} %get-tuple-element.351), channel_id=1, source_target_pairs={{28,0},{0,4},{4,8},{8,12},{12,16},{16,20},{20,24},{24,28},{29,1},{... | collective-permute-start | bytes 18440 | tf_op jit(solution)/shard_map/ppermute | solution.py:20
  212.5 6.5 %collective-permute-start.14 = (f32[3,512]{1,0:T(4,128)S(1)}, f32[3,512]{1,0:T(4,128)S(1)}, u32[]{:S(2)}, u32[]{:S(2)}) collective-permute-start(f32[3,512]{1,0:T(4,128)S(1)} %get-tuple-element.352), channel_id=1, source_target_pairs={{4,0},{8,4},{12,8},{16,12},{20,16},{24,20},{28,24},{0,28},{5,1},{9... | collective-permute-start | bytes 18440 | tf_op jit(solution)/shard_map/ppermute | solution.py:20
  218.6 3.1 collective-permute-start.13
  219.0 26.5 %collective-permute-start.1 = (f32[3,512]{1,0:T(4,128)S(1)}, f32[3,512]{1,0:T(4,128)S(1)}, u32[]{:S(2)}, u32[]{:S(2)}) collective-permute-start(f32[3,512]{1,0:T(4,128)S(1)} %get-tuple-element.342), channel_id=1, source_target_pairs={{1,0},{2,1},{3,2},{0,3},{5,4},{6,5},{7,6},{4,7},{9,8},{10,9},{11,1... | collective-permute-start | bytes 18440 | tf_op jit(solution)/shard_map/ppermute | solution.py:31
  238.7 6.4 %collective-permute-start.16 = (f32[3,512]{1,0:T(4,128)S(1)}, f32[3,512]{1,0:T(4,128)S(1)}, u32[]{:S(2)}, u32[]{:S(2)}) collective-permute-start(f32[3,512]{1,0:T(4,128)S(1)} %get-tuple-element.349), channel_id=1, source_target_pairs={{28,0},{0,4},{4,8},{8,12},{12,16},{16,20},{20,24},{24,28},{29,1},{... | collective-permute-start | bytes 18440 | tf_op jit(solution)/shard_map/ppermute | solution.py:20
  239.2 13.0 %collective-permute-start.18 = (f32[3,512]{1,0:T(4,128)S(1)}, f32[3,512]{1,0:T(4,128)S(1)}, u32[]{:S(2)}, u32[]{:S(2)}) collective-permute-start(f32[3,512]{1,0:T(4,128)S(1)} %get-tuple-element.350), channel_id=1, source_target_pairs={{4,0},{8,4},{12,8},{16,12},{20,16},{24,20},{28,24},{0,28},{5,1},{9... | collective-permute-start | bytes 18440 | tf_op jit(solution)/shard_map/ppermute | solution.py:20
  245.1 8.5 %collective-permute-start.17 = (f32[3,512]{1,0:T(4,128)S(1)}, f32[3,512]{1,0:T(4,128)S(1)}, u32[]{:S(2)}, u32[]{:S(2)}) collective-permute-start(f32[3,512]{1,0:T(4,128)S(1)} %collective-permute-done.16), channel_id=1, source_target_pairs={{3,0},{0,1},{1,2},{2,3},{7,4},{4,5},{5,6},{6,7},{11,8},{8,9},{9,10... | collective-permute-start | bytes 18440 | tf_op jit(solution)/shard_map/ppermute | solution.py:20
  252.2 2.8 collective-permute-start.19
  270.7 6.5 %collective-permute-start.20 = (f32[3,512]{1,0:T(4,128)S(1)}, f32[3,512]{1,0:T(4,128)S(1)}, u32[]{:S(2)}, u32[]{:S(2)}) collective-permute-start(f32[3,512]{1,0:T(4,128)S(1)} %get-tuple-element.347), channel_id=1, source_target_pairs={{28,0},{0,4},{4,8},{8,12},{12,16},{16,20},{20,24},{24,28},{29,1},{... | collective-permute-start | bytes 18440 | tf_op jit(solution)/shard_map/ppermute | solution.py:20
  272.5 91.9 %collective-permute-start.22 = (f32[3,512]{1,0:T(4,128)S(1)}, f32[3,512]{1,0:T(4,128)S(1)}, u32[]{:S(2)}, u32[]{:S(2)}) collective-permute-start(f32[3,512]{1,0:T(4,128)S(1)} %get-tuple-element.348), channel_id=1, source_target_pairs={{4,0},{8,4},{12,8},{16,12},{20,16},{24,20},{28,24},{0,28},{5,1},{9... | collective-permute-start | bytes 18440 | tf_op jit(solution)/shard_map/ppermute | solution.py:20
  277.2 88.0 %collective-permute-start.21 = (f32[3,512]{1,0:T(4,128)S(1)}, f32[3,512]{1,0:T(4,128)S(1)}, u32[]{:S(2)}, u32[]{:S(2)}) collective-permute-start(f32[3,512]{1,0:T(4,128)S(1)} %collective-permute-done.20), channel_id=1, source_target_pairs={{3,0},{0,1},{1,2},{2,3},{7,4},{4,5},{5,6},{6,7},{11,8},{8,9},{9,10... | collective-permute-start | bytes 18440 | tf_op jit(solution)/shard_map/ppermute | solution.py:20
  364.4 2.2 collective-permute-start.23
  (6 other events, 282.2 us)
Sparse Core Ops, SparseCore 0:
  13.5 151.6 reduce-scatter.3
where the time goes:
time: 424 us; the launch traced here: 422 us
  waiting for transfers between devices  158 us (37%)
  other arithmetic  127 us (30%)
  local copies, waits for them, and re-layouts  49.4 us (12%)
  starting transfers between devices  39.8 us (9%)
  blocking collectives  30.7 us (7%)
  between operations  14.7 us (3%)
    unnamed x2, waiting for transfers between devices  145 us
    all_gather x1, blocking collectives, per_device(): pulled = lax.all_gather(pulled_own, 'bead', axis=1, tiled=True)  30.7 us
    ppermute x20, starting transfers between devices, shifted(): return lax.ppermute(block, axis, route)  30.6 us
    reduce_sum x32, other arithmetic, repulsion_kernel(): return REPULSION * jnp.sum(weight[None] * displace, axis=3)  27.5 us
    sub x64, local copies, waits for them, and re-layouts, repulsion_kernel(): displace = targets[:, :, :, None] - sources[:, :, None, :]  25.9 us
    reduce_sum x16, other arithmetic, dipole_kernel(): jnp.sum(weight[None] * (0.25 * displace * projected[None] - 0.5 * spread_...  24.9 us
    reduce_sum x32, other arithmetic, repulsion_kernel(): weight = jnp.exp(-0.5 * jnp.sum(displace * displace, axis=0))  22.1 us
    reduce_sum x16, other arithmetic, dipole_kernel(): weight = jnp.exp(-0.25 * jnp.sum(displace * displace, axis=0))  16.8 us
  transfers between devices with their start and end apart: 25, of which 14 were waited for; matrix products, arithmetic and copies ran while one was open for 40% of the time, Pallas kernels for 0%

commit v1 on v0

v1 whole, which is shorter than its diff:
```python
import functools

import jax
import jax.numpy as jnp
from jax import lax
from jax.experimental import pallas as pl
from jax.experimental.pallas import tpu as pltpu
from jax.sharding import PartitionSpec as P

TILE = 128
NBR = 8
HALO_T = 4
ITERS = 3
REPULSION = 0.2
SPRING = 0.1
LOG2E = 1.4426950408889634
SHORT_K = 0.5 * LOG2E
CENT_K = 0.25 * LOG2E
F32 = jnp.float32
BF16 = jnp.bfloat16
VMEM = pl.BlockSpec(memory_space=pltpu.VMEM)
SMEM = pl.BlockSpec(memory_space=pltpu.SMEM)


def at(tile):
    return pl.ds(pl.multiple_of(tile * TILE, TILE), TILE)


def rows(block):
    return lax.broadcasted_iota(jnp.int32, block.shape, 0)


def pieces(block, count):
    parts = []
    for _ in range(count):
        top = block.astype(BF16).astype(F32)
        parts.append(top)
        block = block - top
    return parts


def target_features(points, k):
    row, norm = rows(points), jnp.sum(points * points, axis=0, keepdims=True)
    high, mid, low = pieces(jnp.where(row == 3, -k * norm, jnp.where(row == 4, 1.0, points)), 3)
    return jnp.concatenate([high, high, mid, mid, high, low], axis=0).astype(BF16)


def source_features(points, k):
    row, norm = rows(points), jnp.sum(points * points, axis=0, keepdims=True)
    high, mid, low = pieces(
        jnp.where(row == 3, 1.0, jnp.where(row == 4, -k * norm, 2 * k * points)), 3
    )
    return jnp.concatenate([high, mid, high, mid, low, high], axis=0).astype(BF16)


def two_parts(block):
    return jnp.concatenate(pieces(block, 2), axis=0).astype(BF16)


def missing_tile(near, row):
    total = sum(range(2 * HALO_T + 1))
    for n in range(NBR):
        total = total - (near[row, n] - row)
    return total


def listed_tile(ref, t, n, missing):
    if n == 0:
        return ref[:, at(t)]
    if n == NBR - 1:
        return ref[:, at(t + NBR)]
    return lax.select(n < missing, ref[:, at(t + n)], ref[:, at(t + n + 1)])


def side_by_side(ref, t, n, missing):
    return jnp.concatenate(
        [listed_tile(ref, t, n, missing), listed_tile(ref, t, n + 1, missing)], axis=1
    )


def pair_weights(sources, target):
    power = lax.dot_general(
        sources, target, (((0,), (0,)), ((), ())), preferred_element_type=F32
    )
    weight = jnp.exp2(power)
    high = weight.astype(BF16)
    return high, (weight - high.astype(F32)).astype(BF16)


def weighted(values, high, low):
    return jnp.dot(values, high, preferred_element_type=F32) + jnp.dot(
        values, low, preferred_element_type=F32
    )


def joined(total):
    half = total.shape[0] // 2
    return total[:half] + total[half:]


def unrolled(count, step, body):
    while count % step:
        step //= 2

    def group(g, carry):
        for u in range(step):
            body(g * step + u)
        return carry

    lax.fori_loop(0, count // step, group, 0)


def fill_points(wide, points):
    wide[...] = jnp.zeros_like(wide)
    wide[0:3, :] = points


def short_prepare(e, wide, features, values):
    points = wide[:, at(e)]
    features[:, at(e)] = source_features(points, SHORT_K)
    values[:, at(e)] = two_parts(jnp.where(rows(points) == 3, 1.0, points))


def short_tile(t, missing, wide, features, values):
    points = wide[:, at(t + HALO_T)]
    target = target_features(points, SHORT_K)
    total = jnp.zeros((16, TILE), F32)
    for n in range(0, NBR, 2):
        high, low = pair_weights(side_by_side(features, t, n, missing), target)
        total = total + weighted(side_by_side(values, t, n, missing), high, low)
    total = joined(total)
    return REPULSION * (points * total[3:4] - total)


def field_values(e, cent, dip, values):
    points, moment = cent[:, at(e)], dip[:, at(e)]
    row = rows(points)
    along = jnp.sum(points * moment, axis=0, keepdims=True)
    block = jnp.where(row == 3, along, moment)
    block = block + pltpu.roll(block, 4, 0)
    first = block * jnp.where(row < 4, 1.0, points[0:1])
    second = block * jnp.where(row < 4, points[1:2], points[2:3])
    values[:, at(e)] = two_parts(jnp.concatenate([first, second], axis=0))


def field_tile(t, missing, cent, values, g_high, g_low):
    total = jnp.zeros((32, TILE), F32)
    for n in range(0, NBR, 2):
        kept = pl.ds(pl.multiple_of((t * NBR + n) * TILE, 2 * TILE), 2 * TILE)
        total = total + weighted(side_by_side(values, t, n, missing), g_high[kept, :], g_low[kept, :])
    total = joined(total)
    points = cent[:, at(t + HALO_T)]
    row = rows(points)
    signed = jnp.where(row == 3, -1.0, points)
    signed = signed + pltpu.roll(signed, 4, 0)
    first, second = signed * total[0:8], signed * total[8:16]

    def low_rows(block):
        return jnp.sum(jnp.where(row < 4, block, 0.0), axis=0, keepdims=True)

    def high_rows(block):
        return jnp.sum(jnp.where(row < 4, 0.0, block), axis=0, keepdims=True)

    turned = jnp.where(
        row == 0, high_rows(first), jnp.where(row == 1, low_rows(second), high_rows(second))
    )
    field = 0.25 * (points * low_rows(first) - turned) - 0.5 * total[0:8]
    return jnp.where(row < 3, field, 0.0)


def cent_prepare(e, cent, charge, features, values):
    points = cent[:, at(e)]
    features[:, at(e)] = source_features(points, CENT_K)
    values[:, at(e)] = two_parts(jnp.where(rows(points) == 3, 1.0, points) * charge[:, at(e)])


def permanent_tile(t, missing, cent, features, values, g_high, g_low):
    points = cent[:, at(t + HALO_T)]
    target = target_features(points, CENT_K)
    total = jnp.zeros((16, TILE), F32)
    for n in range(0, NBR, 2):
        kept = pl.ds(pl.multiple_of((t * NBR + n) * TILE, 2 * TILE), 2 * TILE)
        high, low = pair_weights(side_by_side(features, t, n, missing), target)
        g_high[kept, :] = high
        g_low[kept, :] = low
        total = total + weighted(side_by_side(values, t, n, missing), high, low)
    total = joined(total)
    return jnp.where(rows(points) < 3, points * total[3:4] - total, 0.0)


def step_kernel(
    beads, spaces, near, pos, charge, alpha, masses, out, dip_out,
    ext, wide, features, values, charge_ext, cent, cent_charge, cent_features, cent_values,
    dip, dip_values, g_high, g_low, permanent, moments, pull_own,
    halo_in, charge_in, spring_in, share_in, rim_in, pull_in,
    halo_send, halo_recv, charge_send, charge_recv, spring_send, spring_recv,
    share_send, share_recv, rim_send, rim_recv, pull_send, pull_recv,
):
    length = pos.shape[1]
    tiles, rim = length // TILE, HALO_T * TILE
    own_tiles = tiles // beads
    own = own_tiles * TILE
    bead, space = lax.axis_index("bead"), lax.axis_index("space")
    base = bead * own_tiles

    def send(source, target, send_sem, recv_sem, where):
        copy = pltpu.make_async_remote_copy(
            src_ref=source, dst_ref=target, send_sem=send_sem, recv_sem=recv_sem,
            device_id=where, device_id_type=pl.DeviceIdType.MESH,
        )
        copy.start()
        return copy

    def bead_at(distance):
        return (lax.rem(bead + distance + beads, beads), space)

    def space_at(distance):
        return (bead, lax.rem(space + distance + spaces, spaces))

    following = (lax.rem(bead + 1, beads), lax.rem(space + (bead + 1) // beads, spaces))
    behind = bead + beads - 1
    preceding = (lax.rem(behind, beads), lax.rem(space + spaces + behind // beads - 1, spaces))

    edges = ((pl.ds(length - rim, rim), 1), (pl.ds(0, rim), -1))
    halos = []
    for side, (edge, way) in enumerate(edges):
        halos.append(send(pos.at[:, edge], halo_in.at[side], halo_send.at[side], halo_recv.at[side], space_at(way)))
        halos.append(send(charge.at[:, edge], charge_in.at[side], charge_send.at[side], charge_recv.at[side], space_at(way)))

    def copy_own(t):
        ext[:, at(t + HALO_T)] = pos[:, at(t)]
        charge_ext[:, at(t + HALO_T)] = charge[:, at(t)]

    unrolled(tiles, 8, copy_own)
    for copy in halos:
        copy.wait()
    for side, start in enumerate((0, length + rim)):
        ext[:, start : start + rim] = halo_in[side]
        charge_ext[:, start : start + rim] = charge_in[side]
    shares = []
    for o in range(1, beads):
        peer = bead_at(o)
        part = pl.ds(pl.multiple_of(peer[0] * own, TILE), own + 2 * rim)
        shares.append(send(ext.at[:, part], share_in.at[o - 1], share_send.at[o - 1], share_recv.at[o - 1], peer))
    springs = [
        send(pos, spring_in.at[side], spring_send.at[side], spring_recv.at[side], bead_at(way))
        for side, way in enumerate((1, -1))
    ]
    fill_points(wide, ext[...])
    unrolled(tiles + 2 * HALO_T, 4, lambda e: short_prepare(e, wide, features, values))

    def short_part(start, count):
        def body(i):
            t = start + i
            out[:, at(t)] = short_tile(t, missing_tile(near, t), wide, features, values)[0:3]

        unrolled(count, 4, body)

    piece = max(tiles // 8, 1)
    rounds = ITERS + 1
    first = tiles - (rounds + 1) * piece
    short_part(0, first)
    for copy in shares:
        copy.wait()
    cent[...] = jnp.zeros_like(cent)
    dip[...] = jnp.zeros_like(dip)

    def center(e):
        total = ext[:, at(base + e)]
        for o in range(1, beads):
            total = total + share_in[o - 1, :, at(e)]
        cent[0:3, at(e)] = total / beads
        cent_charge[:, at(e)] = charge_ext[:, at(base + e)]

    def local_missing(t):
        return missing_tile(near, base + t)

    unrolled(own_tiles + 2 * HALO_T, 4, center)
    unrolled(
        own_tiles + 2 * HALO_T, 4,
        lambda e: cent_prepare(e, cent, cent_charge, cent_features, cent_values),
    )

    def start_tile(t):
        found = permanent_tile(t, local_missing(t), cent, cent_features, cent_values, g_high, g_low)[0:3]
        permanent[:, at(t)] = found
        moments[0, :, at(t)] = alpha[:, at(base + t)] * found

    unrolled(own_tiles, 4, start_tile)

    def sweep(r, carry):
        copies = [
            send(moments.at[r, :, pl.ds(own - rim, rim)], rim_in.at[r, 0], rim_send.at[r, 0], rim_recv.at[r, 0], following),
            send(moments.at[r, :, pl.ds(0, rim)], rim_in.at[r, 1], rim_send.at[r, 1], rim_recv.at[r, 1], preceding),
        ]
        short_part(first + r * piece, piece)

        def own_moment(t):
            dip[0:3, at(t + HALO_T)] = moments[r, :, at(t)]

        unrolled(own_tiles, 4, own_moment)
        for copy in copies:
            copy.wait()
        dip[0:3, 0:rim] = rim_in[r, 0]
        dip[0:3, rim + own : 2 * rim + own] = rim_in[r, 1]
        unrolled(own_tiles + 2 * HALO_T, 4, lambda e: field_values(e, cent, dip, dip_values))

        def field(t):
            found = field_tile(t, local_missing(t), cent, dip_values, g_high, g_low)[0:3]
            moments[r + 1, :, at(t)] = alpha[:, at(base + t)] * (permanent[:, at(t)] + found)
            pull_own[:, at(t)] = charge[:, at(base + t)] * found

        unrolled(own_tiles, 4, field)
        return carry

    lax.fori_loop(0, rounds, sweep, 0)
    pulls = [
        send(pull_own, pull_in.at[o - 1], pull_send.at[o - 1], pull_recv.at[o - 1], bead_at(o))
        for o in range(1, beads)
    ]
    dip_out[...] = moments[ITERS]
    short_part(tiles - piece, piece)
    for copy in springs:
        copy.wait()

    def spring(t):
        own_at = at(t)
        bent = spring_in[0, :, own_at] + spring_in[1, :, own_at] - 2.0 * pos[:, own_at]
        out[:, own_at] = out[:, own_at] + SPRING * masses[:, own_at] * bent

    unrolled(tiles, 8, spring)
    for copy in pulls:
        copy.wait()

    def add_pull(t):
        out[:, at(base + t)] = out[:, at(base + t)] + pull_own[:, at(t)]
        for o in range(1, beads):
            from_tile = lax.rem(bead - o + beads, beads) * own_tiles
            out[:, at(from_tile + t)] = out[:, at(from_tile + t)] + pull_in[o - 1, :, at(t)]

    unrolled(own_tiles, 1, add_pull)


def shaped(*shape):
    return jax.ShapeDtypeStruct(shape, F32)


def per_device(positions, charges, polarizability, masses, neighbors):
    length = positions.shape[2]
    beads, spaces = lax.axis_size("bead"), lax.axis_size("space")
    rim = HALO_T * TILE
    own = length // beads
    full, wide, kept = length + 2 * rim, own + 2 * rim, own * NBR
    peers, rounds = beads - 1, ITERS + 1
    dma = pltpu.SemaphoreType.DMA
    forces, dipoles = pl.pallas_call(
        functools.partial(step_kernel, beads, spaces),
        out_shape=(shaped(3, length), shaped(3, own)),
        in_specs=[SMEM] + [VMEM] * 4,
        out_specs=(VMEM, VMEM),
        scratch_shapes=[
            pltpu.VMEM((3, full), F32),
            pltpu.VMEM((8, full), F32),
            pltpu.VMEM((48, full), BF16),
            pltpu.VMEM((16, full), BF16),
            pltpu.VMEM((1, full), F32),
            pltpu.VMEM((8, wide), F32),
            pltpu.VMEM((1, wide), F32),
            pltpu.VMEM((48, wide), BF16),
            pltpu.VMEM((16, wide), BF16),
            pltpu.VMEM((8, wide), F32),
            pltpu.VMEM((32, wide), BF16),
            pltpu.VMEM((kept, TILE), BF16),
            pltpu.VMEM((kept, TILE), BF16),
            pltpu.VMEM((3, own), F32),
            pltpu.VMEM((rounds + 1, 3, own), F32),
            pltpu.VMEM((3, own), F32),
            pltpu.VMEM((2, 3, rim), F32),
            pltpu.VMEM((2, 1, rim), F32),
            pltpu.VMEM((2, 3, length), F32),
            pltpu.VMEM((peers, 3, wide), F32),
            pltpu.VMEM((rounds, 2, 3, rim), F32),
            pltpu.VMEM((peers, 3, own), F32),
            dma((2,)), dma((2,)), dma((2,)), dma((2,)), dma((2,)), dma((2,)),
            dma((peers,)), dma((peers,)), dma((rounds, 2)), dma((rounds, 2)), dma((peers,)), dma((peers,)),
        ],
        compiler_params=pltpu.CompilerParams(vmem_limit_bytes=48 << 20, has_side_effects=True),
    )(neighbors, positions[0], charges[None], polarizability[None], masses[None])
    return forces[None], dipoles


def solution(mesh):
    in_specs = (P("bead", None, "space"), P("space"), P("space"), P("space"), P("space", None))
    out_specs = (P("bead", None, "space"), P(None, ("space", "bead")))
    return jax.shard_map(
        per_device, mesh=mesh, in_specs=in_specs, out_specs=out_specs, check_vma=False
    )
```

time: 424 us -> 66.6 us (0.16)
  waiting for transfers between devices: 158 us -> 0 us
  other arithmetic: 127 us -> 0 us
  Pallas kernels: 0 us -> 62.3 us
  local copies, waits for them, and re-layouts: 49.4 us -> 3.4 us
  starting transfers between devices: 39.8 us -> 0 us
  blocking collectives: 30.7 us -> 0 us
  between operations: 14.7 us -> 0.69 us
    unnamed x2 -> x0, waiting for transfers between devices: 145 us -> none
    reduce_sum x104 -> x0, other arithmetic: 97.6 us -> none  [the longest x32 27.5 us: repulsion_kernel(): return REPULSION * jnp.sum(weight[None] * displace, axis=3)]
    pallas_call x0 -> x1, Pallas kernels: none -> 62.3 us  [per_device(): pl.pallas_call(functools.partial(step_kernel, beads, spaces), out_shape=(...]
    ppermute x24 -> x0, starting transfers between devices: 39.7 us -> none  [the longest x20 30.6 us: shifted(): return lax.ppermute(block, axis, route)]
    all_gather x1 -> x0, blocking collectives: 30.7 us -> none  [per_device(): pulled = lax.all_gather(pulled_own, 'bead', axis=1, tiled=True)]
    sub x104 -> x0, local copies, waits for them, and re-layouts: 26.4 us -> none  [the longest x64 25.9 us: repulsion_kernel(): displace = targets[:, :, :, None] - sources[:, :, None, :]]
    exp x48 -> x0, other arithmetic: 23.8 us -> none  [the longest x16 14.8 us: dipole_kernel(): weight = jnp.exp(-0.25 * jnp.sum(displace * displace, axis=0))]
    ppermute x24 -> x0, waiting for transfers between devices: 12.9 us -> none  [the longest x20 12.9 us: shifted(): return lax.ppermute(block, axis, route)]
  transfers between devices with their start and end apart: 25 -> 0, of which waited for: 14 -> 0; matrix products, arithmetic and copies ran while one was open for 40% -> 0% of each run, Pallas kernels for 0% -> 0%
where the time goes in v1:
time: 66.6 us; the launch traced here: 66.4 us
  Pallas kernels  62.3 us (94%)
  local copies, waits for them, and re-layouts  3.4 us (5%)
  between operations  0.69 us (1%)
    pallas_call x1, Pallas kernels, per_device(): pl.pallas_call(functools.partial(step_kernel, beads, spaces), out_shape=(...  62.3 us
    unnamed x12, local copies, waits for them, and re-layouts  3.4 us

profile of v1, /device:TPU:0, one launch (start us, length us, event | category | flops | bytes accessed | tf_op | source)
XLA Modules:
  0.0 66.4 jit_solution(14907945229768918502)
XLA Ops:
  0.6 0.0 copy-start.3
  0.6 0.7 %copy-done.3 = s32[128,8]{0,1:T(8,128)S(1)} copy-done((s32[128,8]{0,1:T(8,128)S(1)}, s32[128,8]{0,1:T(8,128)}, u32[]{:S(2)}) %copy-start.3) | copy-done | bytes 4120
  1.3 0.1 copy.7.near
  1.4 0.0 copy-start
  1.4 0.0 copy-start.1
  1.4 0.0 copy-start.2
  1.4 1.1 %copy.11 = f32[1,3,16384]{2,1,0:T(4,128)S(1)} copy(f32[1,3,16384]{2,0,1:T(1,128)} %param.5) | data formatting | bytes 393216
  2.6 0.0 copy-done
  2.6 0.0 copy-done.1
  2.6 0.0 copy-done.2
  2.6 62.3 %shard_map.68 = (f32[3,16384]{1,0:T(4,128)S(1)}, f32[3,2048]{1,0:T(4,128)S(1)}) custom-call(s32[128,8]{1,0:T(8,128)S(1)} %copy.7.near, f32[3,16384]{1,0:T(4,128)S(1)} %bitcast.7, f32[1,16384]{1,0:T(1,128)S(1)} %bitcast.9, f32[1,16384]{1,0:T(1,128)S(1)} %bitcast.10, f32[1,16384]{1,0:T(1,128)S(1)} %bitcast.11), custom_call_target="tpu_custom_call" | custom-call | tf_op jit(solution)/shard_map/pallas_call | solution.py:356
  64.9 0.9 %copy.8 = f32[1,3,16384]{2,0,1:T(1,128)} copy(f32[1,3,16384]{2,1,0:T(4,128)S(1)} %bitcast.8) | data formatting | bytes 393216
  65.8 0.6 copy.13
Async XLA Ops:
  0.6 0.7 %copy-start.3 = (s32[128,8]{0,1:T(8,128)S(1)}, s32[128,8]{0,1:T(8,128)}, u32[]{:S(2)}) copy-start(s32[128,8]{0,1:T(8,128)} %param.9) | copy-start | bytes 12292
  1.4 1.1 %copy-start = (f32[16384]{0:T(1024)S(1)}, f32[16384]{0:T(1024)}, u32[]{:S(2)}) copy-start(f32[16384]{0:T(1024)} %param.6) | copy-start | bytes 196612
  1.4 1.1 %copy-start.1 = (f32[16384]{0:T(1024)S(1)}, f32[16384]{0:T(1024)}, u32[]{:S(2)}) copy-start(f32[16384]{0:T(1024)} %param.7) | copy-start | bytes 196612
  1.4 1.1 %copy-start.2 = (f32[16384]{0:T(1024)S(1)}, f32[16384]{0:T(1024)}, u32[]{:S(2)}) copy-start(f32[16384]{0:T(1024)} %param.8) | copy-start | bytes 196612

commit v2 on v1

--- a/solution.py
+++ b/solution.py
@@ -247,14 +247,14 @@
         for side, way in enumerate((1, -1))
     ]
     fill_points(wide, ext[...])
-    unrolled(tiles + 2 * HALO_T, 4, lambda e: short_prepare(e, wide, features, values))
+    unrolled(tiles + 2 * HALO_T, 8, lambda e: short_prepare(e, wide, features, values))
 
     def short_part(start, count):
         def body(i):
             t = start + i
             out[:, at(t)] = short_tile(t, missing_tile(near, t), wide, features, values)[0:3]
 
-        unrolled(count, 4, body)
+        unrolled(count, 16, body)
 
     piece = max(tiles // 8, 1)
     rounds = ITERS + 1
@@ -275,9 +275,9 @@
     def local_missing(t):
         return missing_tile(near, base + t)
 
-    unrolled(own_tiles + 2 * HALO_T, 4, center)
+    unrolled(own_tiles + 2 * HALO_T, 8, center)
     unrolled(
-        own_tiles + 2 * HALO_T, 4,
+        own_tiles + 2 * HALO_T, 8,
         lambda e: cent_prepare(e, cent, cent_charge, cent_features, cent_values),
     )
 
@@ -286,7 +286,7 @@
         permanent[:, at(t)] = found
         moments[0, :, at(t)] = alpha[:, at(base + t)] * found
 
-    unrolled(own_tiles, 4, start_tile)
+    unrolled(own_tiles, 16, start_tile)
 
     def sweep(r, carry):
         copies = [
@@ -303,14 +303,14 @@
             copy.wait()
         dip[0:3, 0:rim] = rim_in[r, 0]
         dip[0:3, rim + own : 2 * rim + own] = rim_in[r, 1]
-        unrolled(own_tiles + 2 * HALO_T, 4, lambda e: field_values(e, cent, dip, dip_values))
+        unrolled(own_tiles + 2 * HALO_T, 8, lambda e: field_values(e, cent, dip, dip_values))
 
         def field(t):
             found = field_tile(t, local_missing(t), cent, dip_values, g_high, g_low)[0:3]
             moments[r + 1, :, at(t)] = alpha[:, at(base + t)] * (permanent[:, at(t)] + found)
             pull_own[:, at(t)] = charge[:, at(base + t)] * found
 
-        unrolled(own_tiles, 4, field)
+        unrolled(own_tiles, 16, field)
         return carry
 
     lax.fori_loop(0, rounds, sweep, 0)
@@ -338,7 +338,7 @@
             from_tile = lax.rem(bead - o + beads, beads) * own_tiles
             out[:, at(from_tile + t)] = out[:, at(from_tile + t)] + pull_in[o - 1, :, at(t)]
 
-    unrolled(own_tiles, 1, add_pull)
+    unrolled(own_tiles, 4, add_pull)
 
 
 def shaped(*shape):

time: 66.6 us -> 90 us (1.35)
  Pallas kernels: 62.3 us -> 85.7 us
    pallas_call x1, Pallas kernels: 62.3 us -> 85.7 us  [per_device(): pl.pallas_call(functools.partial(step_kernel, beads, spaces), out_shape=(...]
where the time goes in v2:
time: 90 us; the launch traced here: 89.8 us
  Pallas kernels  85.7 us (95%)
  local copies, waits for them, and re-layouts  3.4 us (4%)
    pallas_call x1, Pallas kernels, per_device(): pl.pallas_call(functools.partial(step_kernel, beads, spaces), out_shape=(...  85.7 us
    unnamed x12, local copies, waits for them, and re-layouts  3.4 us

profile of v2, /device:TPU:0, one launch (start us, length us, event | category | flops | bytes accessed | tf_op | source)
XLA Modules:
  0.0 89.8 jit_solution(5276089428239612245)
XLA Ops:
  0.6 0.0 copy-start.3
  0.6 0.7 copy-done.3
  1.3 0.1 copy.7.near
  1.4 0.0 copy-start
  1.4 0.0 copy-start.1
  1.4 0.0 copy-start.2
  1.4 1.1 %copy.11 = f32[1,3,16384]{2,1,0:T(4,128)S(1)} copy(f32[1,3,16384]{2,0,1:T(1,128)} %param.5) | data formatting | bytes 393216
  2.6 0.0 copy-done
  2.6 0.0 copy-done.1
  2.6 0.0 copy-done.2
  2.6 85.7 %shard_map.68 = (f32[3,16384]{1,0:T(4,128)S(1)}, f32[3,2048]{1,0:T(4,128)S(1)}) custom-call(s32[128,8]{1,0:T(8,128)S(1)} %copy.7.near, f32[3,16384]{1,0:T(4,128)S(1)} %bitcast.7, f32[1,16384]{1,0:T(1,128)S(1)} %bitcast.9, f32[1,16384]{1,0:T(1,128)S(1)} %bitcast.10, f32[1,16384]{1,0:T(1,128)S(1)} %bitcast.11), custom_call_target="tpu_custom_call" | custom-call | tf_op jit(solution)/shard_map/pallas_call | solution.py:356
  88.3 0.9 copy.8
  89.2 0.6 copy.13
Async XLA Ops:
  0.6 0.7 copy-start.3
  1.4 1.1 %copy-start = (f32[16384]{0:T(1024)S(1)}, f32[16384]{0:T(1024)}, u32[]{:S(2)}) copy-start(f32[16384]{0:T(1024)} %param.6) | copy-start | bytes 196612
  1.4 1.1 %copy-start.1 = (f32[16384]{0:T(1024)S(1)}, f32[16384]{0:T(1024)}, u32[]{:S(2)}) copy-start(f32[16384]{0:T(1024)} %param.7) | copy-start | bytes 196612
  1.4 1.1 %copy-start.2 = (f32[16384]{0:T(1024)S(1)}, f32[16384]{0:T(1024)}, u32[]{:S(2)}) copy-start(f32[16384]{0:T(1024)} %param.8) | copy-start | bytes 196612
